TPU v7x, 32 devices: a whole 2x2x4 slice. The times are simulated.
32 devices in a mesh: grid: 8 (over y, x, core), orb: 4 (over z).
Axes of the slice: x: 2, y: 2, z: 4, core: 2. Of those that a mesh axis runs over, the one named last changes fastest.
Arguments:
- psi_in: float32 [128, 48, 8, 128], P('orb', 'grid')
- v_local: float32 [48, 8, 128], P('grid'), may hold values from -3 to 0.5
- proj_index: int32 [24, 4, 128], P('grid'), may hold values from 0 to 6143
- proj_value: float32 [24, 4, 4, 128], P('grid'), may hold values from -1.2 to 1.2
- kb_energy: float32 [32, 4], P('grid'), may hold values from 0.5 to 3
Outputs:
- filtered: float32 [128, 48, 8, 128], P('orb', 'grid')
- gram: float32 [128, 128], P('orb', 'grid')
All inputs are finite; a program needn't handle non-finite values.
Results may differ from a plain program's by a relative error of at most 0.00005.
Values sent between devices are 32-bit elements; how exact they have to be, the bound alone decides.
A program may use at most 128 MiB of HBM per device.

v0:
```python
import jax
import jax.numpy as jnp
from jax import lax
from jax.sharding import PartitionSpec as P

LAP_COEF = (
    -5369.0 / 1800.0,
    12.0 / 7.0,
    -15.0 / 56.0,
    10.0 / 189.0,
    -1.0 / 112.0,
    2.0 / 1925.0,
    -1.0 / 16632.0,
)
HIGH = lax.Precision.HIGHEST


def with_halo(cells, sides, width):
    for axis, dim in sides:
        count = lax.axis_size(axis)
        head = lax.slice_in_dim(cells, 0, width, axis=dim)
        tail = lax.slice_in_dim(cells, cells.shape[dim] - width, cells.shape[dim], axis=dim)
        cells = jnp.concatenate(
            [
                lax.ppermute(tail, axis, [(i, (i + 1) % count) for i in range(count)]),
                cells,
                lax.ppermute(head, axis, [((i + 1) % count, i) for i in range(count)]),
            ],
            axis=dim,
        )
    return cells


def nonlocal_part(field, proj_index, proj_value, kb_energy):
    orbitals = field.shape[0]
    slots = proj_index.shape[1]
    points = proj_index.shape[2]
    flattened = field.reshape(orbitals, -1)
    columns = proj_index.reshape(-1)
    picked = jnp.take(flattened, columns, axis=1).reshape(orbitals, 3, slots, points)
    partial_value = jnp.einsum("kamp,okap->kamo", proj_value, picked, precision=HIGH)
    outgoing = jnp.stack([partial_value[0], partial_value[2]])
    arrived = with_halo(outgoing, (("grid", 0),), 1)
    summed = partial_value[1] + arrived[0] + arrived[3]
    scaled = summed * kb_energy[:, :, None]
    returned = with_halo(scaled[None], (("grid", 0),), 1)
    contrib = jnp.einsum("kamp,kamo->okap", proj_value, returned, precision=HIGH).reshape(
        orbitals, -1
    )
    result = jnp.zeros_like(flattened).at[:, columns].add(contrib)
    return result.reshape(field.shape)


def hamilton(field, v_local, proj_index, proj_value, kb_energy):
    planes = field.shape[1]
    extended = with_halo(field, (("grid", 1),), 6)
    laplace = 3.0 * LAP_COEF[0] * field
    for offset in range(1, 7):
        upper = extended[:, 6 + offset : 6 + offset + planes]
        lower = extended[:, 6 - offset : 6 - offset + planes]
        laplace = laplace + LAP_COEF[offset] * (upper + lower)
        for axis in (2, 3):
            laplace = laplace + LAP_COEF[offset] * (
                jnp.roll(field, offset, axis) + jnp.roll(field, -offset, axis)
            )
    return (
        -0.5 * laplace
        + v_local[None] * field
        + nonlocal_part(field, proj_index, proj_value, kb_energy)
    )


def on_device(psi_in, v_local, proj_index, proj_value, kb_energy):
    half_width = 6.0
    centre = 8.0
    sigma = half_width / (-3.0 - centre)
    sigma_two = 1.0 / (2.0 / sigma - sigma)
    first = (hamilton(psi_in, v_local, proj_index, proj_value, kb_energy) - centre * psi_in) * (
        sigma / half_width
    )
    filtered = (hamilton(first, v_local, proj_index, proj_value, kb_energy) - centre * first) * (
        2.0 * sigma_two / half_width
    ) - sigma * sigma_two * psi_in
    orbitals = filtered.shape[0]
    flattened = filtered.reshape(orbitals, -1)
    cells_total = lax.axis_size("grid") * flattened.shape[1]
    partial_value = lax.dot_general(
        flattened,
        lax.all_gather(flattened, "orb", axis=0, tiled=True),
        (((1,), (1,)), ((), ())),
        precision=HIGH,
        preferred_element_type=jnp.float32,
    )
    owned_tile = lax.psum_scatter(partial_value, "grid", scatter_dimension=1, tiled=True)
    gram = owned_tile / cells_total
    return (filtered, gram)


def solution(mesh):
    placed = (
        P("orb", "grid", None, None),
        P("grid", None, None),
        P("grid", None, None),
        P("grid", None, None, None),
        P("grid", None),
    )
    return jax.shard_map(
        on_device,
        mesh=mesh,
        in_specs=placed,
        out_specs=(P("orb", "grid", None, None), P("orb", "grid")),
        check_vma=False,
    )
```

profile of v0, /device:TPU:0, one launch (start us, length us, event | category | flops | bytes accessed | tf_op | source)
XLA Modules:
  0.0 270.4 jit_solution(10097822072393388637)
XLA Ops:
  7.8 2.9 %collective-permute-start = (f32[32,6,8,128]{3,2,1,0:T(8,128)}, f32[32,6,8,128]{3,2,1,0:T(8,128)S(1)}, u32[]{:S(2)}, u32[]{:S(2)}) collective-permute-start(f32[32,6,8,128]{3,2,1,0:T(8,128)} %param.7), channel_id=1, source_target_pairs={{4,0},{8,4},{12,8},{16,12},{20,16},{24,20},{28,24},{0,28},{5,1},{9... | collective-permute-start | bytes 2359304 | tf_op jit(solution)/shard_map/ppermute | solution.py:27
  10.7 3.1 %copy.13 = f32[32,6,8,128]{0,3,2,1:T(8,128)} copy(f32[32,6,8,128]{3,2,1,0:T(8,128)} %param.7) | data formatting | bytes 1572864 | tf_op args[0]
  13.9 4.5 %gather_fusion = f32[1536,32]{1,0:T(8,128)S(1)} fusion(f32[32,6144]{0,1:T(8,128)} %bitcast.39, s32[2048]{0:T(1024)S(1)} %pad_clamp_fusion), kind=kCustom, calls=%fused_computation.clone | custom fusion | bytes 399360 | tf_op jit(solution)/shard_map/jit(_take)/gather | solution.py:40
  19.5 2.6 collective-permute-start.3
  24.8 1.5 fusion.128
  27.5 1.4 fusion.131
  32.9 1.4 fusion.136
  35.7 1.5 fusion.139
  37.2 1.5 fusion.140
  38.6 1.4 fusion.141
  41.5 1.4 fusion.143
  46.6 2.6 collective-permute-start.5
  53.2 10.5 %scatter_custom_fusion = f32[32,6144]{0,1:T(8,128)} fusion(s32[1536]{0:T(1024)S(1)} %fusion.101, f32[1536,32]{1,0:T(8,128)S(1)} %copy.16, f32[]{:T(128)} %constant.11.clone.1), kind=kCustom, calls=%fused_computation.22 | custom fusion | flops 49152 | bytes 786436 | tf_op jit(solution)/shard_map/scatter-add | solution.py:50
  63.7 3.1 %copy.17 = f32[32,6,8,128]{3,2,1,0:T(8,128)} copy(f32[32,6,8,128]{0,3,2,1:T(8,128)} %bitcast.37) | data formatting | bytes 1572864 | tf_op jit(solution)/shard_map/reshape | solution.py:51
  69.3 10.6 %broadcast_multiply_fusion = (f32[32,6,8,128]{3,2,1,0:T(8,128)S(1)}, f32[32,6,8,128]{3,2,1,0:T(8,128)}) fusion(f32[32,6,8,128]{3,2,1,0:T(8,128)S(1)} %copy-done.1, f32[32,6,8,128]{3,2,1,0:T(8,128)} %copy.17, f32[6,8,128]{2,1,0:T(8,128)S(1)} %copy-done.10, f32[32,6,8,6]{3,2,1,0:T(8,128)} %get-tuple-element.80, f32[32,6,8,122]{3,2,1,0:T(8,128)} %get-tuple-element.82, ...), kind=kLoop, calls=%fused_computation.142 | loop fusion | flops 15532032 | bytes 27549696 | tf_op jit(solution)/shard_map/mul | solution.py:78
  79.9 2.2 copy.18
  83.3 1.4 fusion.109
  87.4 1.4 fusion.113
  92.8 1.5 fusion.119
  95.7 1.5 fusion.121
  99.9 1.4 fusion.124
  104.6 2.6 collective-permute-start.6
  107.2 4.5 %gather_fusion.1 = f32[1536,32]{1,0:T(8,128)S(1)} fusion(f32[32,6144]{0,1:T(8,128)} %bitcast.38, s32[2048]{0:T(1024)S(1)} %pad_clamp_fusion), kind=kCustom, calls=%fused_computation.1.clone | custom fusion | bytes 399360 | tf_op jit(solution)/shard_map/jit(_take)/gather | solution.py:40
  112.8 2.7 collective-permute-start.9
  116.3 9.0 %collective-permute-done.8 = f32[1,4,4,32]{3,2,1,0:T(4,128)S(1)} collective-permute-done((f32[1,4,4,32]{3,2,1,0:T(4,128)S(1)}, f32[1,4,4,32]{3,2,1,0:T(4,128)S(1)}, u32[]{:S(2)}, u32[]{:S(2)}) %collective-permute-start.8) | collective-permute-done | bytes 2080 | tf_op jit(solution)/shard_map/ppermute | solution.py:25
  125.4 2.6 collective-permute-start.11
  132.0 10.5 %scatter_custom_fusion.1 = f32[32,6144]{0,1:T(8,128)} fusion(s32[1536]{0:T(1024)S(1)} %fusion.101, f32[1536,32]{1,0:T(8,128)S(1)} %copy.21, f32[]{:T(128)} %constant.11.clone.1), kind=kCustom, calls=%fused_computation.20 | custom fusion | flops 49152 | bytes 786436 | tf_op jit(solution)/shard_map/scatter-add | solution.py:50
  142.5 3.1 %copy.22 = f32[32,6,8,128]{3,2,1,0:T(8,128)} copy(f32[32,6,8,128]{0,3,2,1:T(8,128)} %bitcast.36) | data formatting | bytes 1572864 | tf_op jit(solution)/shard_map/reshape | solution.py:51
  145.6 13.2 %multiply_subtract_fusion = f32[32,6,8,128]{3,2,1,0:T(8,128)S(1)} fusion(f32[32,6,8,128]{3,2,1,0:T(8,128)S(1)} %copy-done.1, f32[32,6,8,128]{3,2,1,0:T(8,128)} %get-tuple-element.4, f32[32,6,8,128]{3,2,1,0:T(8,128)} %copy.22, f32[32,6,8,6]{3,2,1,0:T(8,128)} %get-tuple-element.40, f32[32,6,8,122]{3,2,1,0:T(8,128)} %get-tuple-element.42, ...), kind=kLoop, calls=%fused_computation.139 | loop fusion | flops 17891328 | bytes 20471808 | tf_op jit(solution)/shard_map/sub | solution.py:81
  160.1 65.1 %all-gather.2.cloned.1.call-done = f32[128,6144]{1,0:T(8,128)} async-done(((f32[32,6144]{1,0:T(8,128)}), f32[128,6144]{1,0:T(8,128)}) %all-gather.2.cloned.1.call-update) | async-done | bytes 3145744 | tf_op jit(solution)/shard_map/all_gather | solution.py:89
  225.2 5.1 %fusion.104 = f32[32,128]{0,1:T(8,128)} fusion(f32[128,6144]{1,0:T(8,128)} %all-gather.2.cloned.1.call-done, f32[4,8,48,128]{3,2,1,0:T(8,128)S(1)} %bitcast.41), kind=kOutput, calls=%fused_computation.172 | convolution fusion | flops 301989888 | bytes 3948544 | tf_op jit(solution)/shard_map/dot_general | solution.py:87
  230.3 32.0 %reduce-scatter.2.cloned.1.call-done = f32[32,16]{0,1:T(8,128)} async-done(((f32[32,128]{0,1:T(8,128)}), f32[32,16]{0,1:T(8,128)}) %reduce-scatter.2.cloned.1.call-update) | async-done | bytes 2064 | tf_op jit(solution)/shard_map/reduce_scatter | solution.py:94
  (100 shorter events, 46.1 us)
Async XLA Ops:
  7.2 11.5 %copy-start = (f32[3,4,4,128]{3,2,1,0:T(4,128)S(1)}, f32[3,4,4,128]{3,2,1,0:T(4,128)}, u32[]{:S(2)}) copy-start(f32[3,4,4,128]{3,2,1,0:T(4,128)} %param.10) | copy-start | bytes 73732
  7.2 14.9 %copy-start.1 = (f32[32,6,8,128]{3,2,1,0:T(8,128)S(1)}, f32[32,6,8,128]{3,2,1,0:T(8,128)}, u32[]{:S(2)}) copy-start(f32[32,6,8,128]{3,2,1,0:T(8,128)} %param.7) | copy-start | bytes 2359300
  7.2 6.7 %copy-start.11 = (s32[3,4,128]{2,1,0:T(4,128)S(1)}, s32[3,4,128]{2,1,0:T(4,128)}, u32[]{:S(2)}) copy-start(s32[3,4,128]{2,1,0:T(4,128)} %param.9) | copy-start | bytes 18436
  7.2 218.0 %all-gather.2.cloned.1.call-start = ((), (), s32[]{:S(2)}) async-start(), calls=%async_computation.1 | async-start | bytes 3932160 | tf_op jit(solution)/shard_map/all_gather | solution.py:89
  7.2 59.6 %collective-permute-start.1 = (f32[32,6,8,128]{3,2,1,0:T(8,128)}, f32[32,6,8,128]{3,2,1,0:T(8,128)S(1)}, u32[]{:S(2)}, u32[]{:S(2)}) collective-permute-start(f32[32,6,8,128]{3,2,1,0:T(8,128)} %param.7), channel_id=1, source_target_pairs={{0,4},{4,8},{8,12},{12,16},{16,20},{20,24},{24,28},{28,0},{1,5},{5... | collective-permute-start | bytes 2359304 | tf_op jit(solution)/shard_map/ppermute | solution.py:25
  7.8 59.3 %collective-permute-start = (f32[32,6,8,128]{3,2,1,0:T(8,128)}, f32[32,6,8,128]{3,2,1,0:T(8,128)S(1)}, u32[]{:S(2)}, u32[]{:S(2)}) collective-permute-start(f32[32,6,8,128]{3,2,1,0:T(8,128)} %param.7), channel_id=1, source_target_pairs={{4,0},{8,4},{12,8},{16,12},{20,16},{24,20},{28,24},{0,28},{5,1},{9... | collective-permute-start | bytes 2359304 | tf_op jit(solution)/shard_map/ppermute | solution.py:27
  19.4 27.0 %collective-permute-start.2 = (f32[1,4,4,32]{3,2,1,0:T(4,128)S(1)}, f32[1,4,4,32]{3,2,1,0:T(4,128)S(1)}, u32[]{:S(2)}, u32[]{:S(2)}) collective-permute-start(f32[1,4,4,32]{3,2,1,0:T(4,128)S(1)} %get-tuple-element.85), channel_id=1, source_target_pairs={{0,4},{4,8},{8,12},{12,16},{16,20},{20,24},{24,28},{28,0},{1,5},{5... | collective-permute-start | bytes 6152 | tf_op jit(solution)/shard_map/ppermute | solution.py:25
  19.5 27.0 %collective-permute-start.3 = (f32[1,4,4,32]{3,2,1,0:T(4,128)S(1)}, f32[1,4,4,32]{3,2,1,0:T(4,128)S(1)}, u32[]{:S(2)}, u32[]{:S(2)}) collective-permute-start(f32[1,4,4,32]{3,2,1,0:T(4,128)S(1)} %get-tuple-element.86), channel_id=1, source_target_pairs={{4,0},{8,4},{12,8},{16,12},{20,16},{24,20},{28,24},{0,28},{5,1},{9... | collective-permute-start | bytes 6152 | tf_op jit(solution)/shard_map/ppermute | solution.py:27
  41.4 5.0 %copy-start.10 = (f32[6,8,128]{2,1,0:T(8,128)S(1)}, f32[6,8,128]{2,1,0:T(8,128)}, u32[]{:S(2)}) copy-start(f32[6,8,128]{2,1,0:T(8,128)} %param.8) | copy-start | bytes 73732
  41.4 5.0 %copy-start.12 = (f32[4,4]{1,0:T(4,128)S(1)}, f32[4,4]{1,0:T(4,128)}, u32[]{:S(2)}) copy-start(f32[4,4]{1,0:T(4,128)} %param.11) | copy-start | bytes 196
  46.5 4.0 %collective-permute-start.4 = (f32[1,4,4,32]{3,2,1,0:T(4,128)S(1)}, f32[1,4,4,32]{3,2,1,0:T(4,128)S(1)}, u32[]{:S(2)}, u32[]{:S(2)}) collective-permute-start(f32[1,4,4,32]{3,2,1,0:T(4,128)S(1)} %fusion.100), channel_id=1, source_target_pairs={{0,4},{4,8},{8,12},{12,16},{16,20},{20,24},{24,28},{28,0},{1,5},{5... | collective-permute-start | bytes 6152 | tf_op jit(solution)/shard_map/ppermute | solution.py:25
  46.6 4.0 %collective-permute-start.5 = (f32[1,4,4,32]{3,2,1,0:T(4,128)S(1)}, f32[1,4,4,32]{3,2,1,0:T(4,128)S(1)}, u32[]{:S(2)}, u32[]{:S(2)}) collective-permute-start(f32[1,4,4,32]{3,2,1,0:T(4,128)S(1)} %fusion.100), channel_id=1, source_target_pairs={{4,0},{8,4},{12,8},{16,12},{20,16},{24,20},{28,24},{0,28},{5,1},{9... | collective-permute-start | bytes 6152 | tf_op jit(solution)/shard_map/ppermute | solution.py:27
  66.8 1.1 copy-start.3
  66.8 1.4 copy-start.4
  66.8 1.6 copy-start.5
  66.8 1.8 copy-start.6
  66.8 2.1 copy-start.7
  66.8 2.3 copy-start.8
  66.8 2.5 copy-start.9
  104.6 41.1 %collective-permute-start.6 = (f32[32,6,8,128]{3,2,1,0:T(8,128)S(1)}, f32[32,6,8,128]{3,2,1,0:T(8,128)}, u32[]{:S(2)}, u32[]{:S(2)}) collective-permute-start(f32[32,6,8,128]{3,2,1,0:T(8,128)S(1)} %get-tuple-element.3), channel_id=1, source_target_pairs={{4,0},{8,4},{12,8},{16,12},{20,16},{24,20},{28,24},{0,28},{5,1},{9... | collective-permute-start | bytes 2359304 | tf_op jit(solution)/shard_map/ppermute | solution.py:27
  107.2 38.4 %collective-permute-start.7 = (f32[32,6,8,128]{3,2,1,0:T(8,128)S(1)}, f32[32,6,8,128]{3,2,1,0:T(8,128)}, u32[]{:S(2)}, u32[]{:S(2)}) collective-permute-start(f32[32,6,8,128]{3,2,1,0:T(8,128)S(1)} %get-tuple-element.3), channel_id=1, source_target_pairs={{0,4},{4,8},{8,12},{12,16},{16,20},{20,24},{24,28},{28,0},{1,5},{5... | collective-permute-start | bytes 2359304 | tf_op jit(solution)/shard_map/ppermute | solution.py:25
  112.7 12.6 %collective-permute-start.8 = (f32[1,4,4,32]{3,2,1,0:T(4,128)S(1)}, f32[1,4,4,32]{3,2,1,0:T(4,128)S(1)}, u32[]{:S(2)}, u32[]{:S(2)}) collective-permute-start(f32[1,4,4,32]{3,2,1,0:T(4,128)S(1)} %get-tuple-element.83), channel_id=1, source_target_pairs={{0,4},{4,8},{8,12},{12,16},{16,20},{20,24},{24,28},{28,0},{1,5},{5... | collective-permute-start | bytes 6152 | tf_op jit(solution)/shard_map/ppermute | solution.py:25
  112.8 12.5 %collective-permute-start.9 = (f32[1,4,4,32]{3,2,1,0:T(4,128)S(1)}, f32[1,4,4,32]{3,2,1,0:T(4,128)S(1)}, u32[]{:S(2)}, u32[]{:S(2)}) collective-permute-start(f32[1,4,4,32]{3,2,1,0:T(4,128)S(1)} %get-tuple-element.84), channel_id=1, source_target_pairs={{4,0},{8,4},{12,8},{16,12},{20,16},{24,20},{28,24},{0,28},{5,1},{9... | collective-permute-start | bytes 6152 | tf_op jit(solution)/shard_map/ppermute | solution.py:27
  125.4 4.0 %collective-permute-start.10 = (f32[1,4,4,32]{3,2,1,0:T(4,128)S(1)}, f32[1,4,4,32]{3,2,1,0:T(4,128)S(1)}, u32[]{:S(2)}, u32[]{:S(2)}) collective-permute-start(f32[1,4,4,32]{3,2,1,0:T(4,128)S(1)} %fusion.98), channel_id=1, source_target_pairs={{0,4},{4,8},{8,12},{12,16},{16,20},{20,24},{24,28},{28,0},{1,5},{5... | collective-permute-start | bytes 6152 | tf_op jit(solution)/shard_map/ppermute | solution.py:25
  125.4 4.0 %collective-permute-start.11 = (f32[1,4,4,32]{3,2,1,0:T(4,128)S(1)}, f32[1,4,4,32]{3,2,1,0:T(4,128)S(1)}, u32[]{:S(2)}, u32[]{:S(2)}) collective-permute-start(f32[1,4,4,32]{3,2,1,0:T(4,128)S(1)} %fusion.98), channel_id=1, source_target_pairs={{4,0},{8,4},{12,8},{16,12},{20,16},{24,20},{28,24},{0,28},{5,1},{9... | collective-permute-start | bytes 6152 | tf_op jit(solution)/shard_map/ppermute | solution.py:27
  158.9 71.4 %copy-start.2 = (f32[32,6,8,128]{3,2,1,0:T(8,128)}, f32[32,6,8,128]{3,2,1,0:T(8,128)S(1)}, u32[]{:S(2)}) copy-start(f32[32,6,8,128]{3,2,1,0:T(8,128)S(1)} %multiply_subtract_fusion) | copy-start | bytes 2359300
  160.0 102.3 %reduce-scatter.2.cloned.1.call-start = ((), (), s32[]{:S(2)}) async-start(), calls=%async_computation.2 | async-start | bytes 73728 | tf_op jit(solution)/shard_map/reduce_scatter | solution.py:94
Sparse Core Ops, SparseCore 0:
  160.1 64.9 all-gather.1
  230.4 31.8 reduce-scatter.1
where the time goes:
time: 271 us; the launch traced here: 270 us
  waiting for transfers between devices  108 us (40%)
  local copies, waits for them, and re-layouts  76.5 us (28%)
  other arithmetic  46.9 us (17%)
  starting transfers between devices  16.8 us (6%)
  between operations  14.3 us (5%)
  matrix products  7.67 us (3%)
    all_gather x1, waiting for transfers between devices, on_device(): lax.all_gather(flattened, 'orb', axis=0, tiled=True)  65.1 us
    slice x38, local copies, waits for them, and re-layouts, hamilton(): jnp.roll(field, offset, axis) + jnp.roll(field, -offset, axis)  48.3 us
    reduce_scatter x1, waiting for transfers between devices, on_device(): lax.psum_scatter(partial_value, 'grid', scatter_dimension=1, tiled=True)  32 us
    scatter-add x2, other arithmetic, nonlocal_part(): result = jnp.zeros_like(flattened).at[:, columns].add(contrib)  21 us
    ppermute x6, starting transfers between devices, with_halo(): lax.ppermute(head, axis, [((i + 1) % count, i) for i in range(count)])  16.2 us
    sub x1, other arithmetic, on_device(): (hamilton(first, v_local, proj_index, proj_value, kb_energy) - centre * f...  13.2 us
    ppermute x6, waiting for transfers between devices, with_halo(): lax.ppermute(tail, axis, [(i, (i + 1) % count) for i in range(count)])  10.9 us
    mul x1, other arithmetic, on_device(): (hamilton(psi_in, v_local, proj_index, proj_value, kb_energy) - centre *...  10.6 us
  transfers between devices with their start and end apart: 14, of which 5 were waited for; matrix products, arithmetic and copies ran while one was open for 27% of the time, Pallas kernels for 0%

commit v1 on v0

v1 whole, which is shorter than its diff:
```python
import functools

import jax
import jax.numpy as jnp
from jax import lax
from jax.experimental import pallas as pl
from jax.experimental.pallas import tpu as pltpu
from jax.sharding import PartitionSpec as P

LAP_COEF = (
    -5369.0 / 1800.0,
    12.0 / 7.0,
    -15.0 / 56.0,
    10.0 / 189.0,
    -1.0 / 112.0,
    2.0 / 1925.0,
    -1.0 / 16632.0,
)
HALF_WIDTH = 6.0
CENTRE = 8.0
SIGMA = HALF_WIDTH / (-3.0 - CENTRE)
SIGMA_TWO = 1.0 / (2.0 / SIGMA - SIGMA)
MESH = pl.DeviceIdType.MESH
OB = 8
KP = 64
PAIR_PARTNERS = (-2, -1, 1, 2)
F32 = jnp.float32
BF16 = jnp.bfloat16
NT = (((1,), (1,)), ((), ()))


def split(x):
    high = x.astype(BF16).astype(F32)
    return high, x - high


def kernel(
    n_grid, n_orb, ny, planes, chunks,
    psi_ref, v_ref, idx_ref, val_ref, kb_ref,
    out_ref, gram_ref,
    ext, pf, pt, fbuf, abuf, ah, gbuf, grecv, sbuf, srecv, pay, prec,
    h_send, h_recv, p_send, p_recv, a_send, a_recv, g_send, g_recv, s_send, s_recv,
):
    rows = ny * planes
    quarter = rows // n_orb
    lanes = 128
    g = lax.axis_index("grid")
    o = lax.axis_index("orb")

    def grid_id(d):
        return lax.rem(g + d + n_grid, n_grid)

    def orb_id(d):
        return lax.rem(o + d, n_orb)

    barrier = pltpu.get_barrier_semaphore()

    @pl.loop(1, n_grid)
    def _(d):
        pl.semaphore_signal(barrier, inc=1, device_id=(grid_id(d), o), device_id_type=MESH)

    for d in range(1, n_orb):
        pl.semaphore_signal(barrier, inc=1, device_id=(g, orb_id(d)), device_id_type=MESH)

    @pl.loop(0, chunks)
    def _(c):
        @pl.loop(0, rows, unroll=8)
        def _(r):
            ext[0, c, rows + r] = psi_ref[pl.ds(c * OB * rows + r, OB, stride=rows), :]

    pl.semaphore_wait(barrier, n_grid - 1 + n_orb - 1)

    def halo(stage, c, side):
        return pltpu.make_async_remote_copy(
            src_ref=ext.at[stage, c, pl.ds(rows, rows)],
            dst_ref=ext.at[stage, c, pl.ds(0 if side == 0 else 2 * rows, rows)],
            send_sem=h_send.at[stage, c, side],
            recv_sem=h_recv.at[stage, c, side],
            device_id=(grid_id(1 if side == 0 else -1), o),
            device_id_type=MESH,
        )

    def partial_copy(stage, c, i):
        return pltpu.make_async_remote_copy(
            src_ref=pay.at[stage, c],
            dst_ref=prec.at[stage, c, i],
            send_sem=p_send.at[stage, c, i],
            recv_sem=p_recv.at[stage, c, i],
            device_id=(grid_id(PAIR_PARTNERS[i]), o),
            device_id_type=MESH,
        )

    @pl.loop(0, chunks)
    def _(c):
        halo(0, c, 0).start()
        halo(0, c, 1).start()

    pf[:, 48:KP, :] = jnp.zeros((rows, KP - 48, lanes), F32)

    @pl.loop(0, 6)
    def _(q):
        value = val_ref[q]
        upper = lax.broadcasted_iota(jnp.int32, (8, lanes), 0) < 4
        value = jnp.concatenate(
            [jnp.where(upper, value, 0.0), jnp.where(upper, 0.0, value)], axis=1
        )
        index = idx_ref[q]
        high = jnp.broadcast_to(index >> 7, (8, 2 * lanes))
        low = jnp.broadcast_to(index & 127, (lanes, 2 * lanes))
        hot = jnp.where(
            lax.broadcasted_iota(jnp.int32, (lanes, 2 * lanes), 0) == low, 1.0, 0.0
        ).astype(BF16)
        vh, vl = split(value)
        left = jnp.concatenate(
            [jnp.where(high == h, vh, 0.0) for h in range(rows)], axis=0
        ).astype(BF16)
        dense = lax.dot_general(left, hot, NT, preferred_element_type=F32)
        left = jnp.concatenate(
            [jnp.where(high == h, vl, 0.0) for h in range(rows)], axis=0
        ).astype(BF16)
        dense = dense + lax.dot_general(left, hot, NT, preferred_element_type=F32)
        pf[:, pl.ds(pl.multiple_of(q * 8, 8), 8), :] = dense.reshape(rows, 8, lanes)

    @pl.loop(0, rows // 2, unroll=2)
    def _(h):
        both = jnp.concatenate([pf[2 * h], pf[2 * h + 1]], axis=1)
        high, low = split(both)
        pt[h] = jnp.concatenate([high, low], axis=0).astype(BF16)

    lane = lax.broadcasted_iota(jnp.int32, (OB, lanes), 1)

    def project(stage, c):
        def step(h, acc):
            both = jnp.concatenate(
                [ext[stage, c, rows + 2 * h], ext[stage, c, rows + 2 * h + 1]], axis=1
            )
            high, low = split(both)
            left = jnp.concatenate([high, low], axis=0).astype(BF16)
            return acc + lax.dot_general(left, pt[h], NT, preferred_element_type=F32)

        acc = lax.fori_loop(0, rows // 2, step, jnp.zeros((2 * OB, lanes), F32), unroll=4)
        total = acc[:OB] + acc[OB:] + pltpu.roll(acc[:OB], 64, 1)
        pay[stage, c] = jnp.where(lane < 48, total, kb_ref[...])
        for i in range(4):
            partial_copy(stage, c, i).start()

    @pl.loop(0, chunks)
    def _(c):
        project(0, c)

    def returned(stage, c):
        for i in range(4):
            partial_copy(stage, c, i).wait_recv()
        above2, above1, below1, below2 = (prec[stage, c, i] for i in range(4))
        own = pay[stage, c]
        total = (
            own
            + jnp.where(lane < 32, pltpu.roll(below1, 112, 1), 0.0)
            + jnp.where(lane >= 16, pltpu.roll(above1, 16, 1), 0.0)
            + jnp.where(lane < 16, pltpu.roll(below2, 96, 1), 0.0)
            + jnp.where(lane >= 32, pltpu.roll(above2, 32, 1), 0.0)
        )
        energy = jnp.where(
            lane < 16,
            pltpu.roll(below1, 64, 1),
            jnp.where(lane < 32, pltpu.roll(own, 80, 1), pltpu.roll(above1, 96, 1)),
        )
        total = jnp.where(lane < 48, total * energy, 0.0)
        high, low = split(total)
        return jnp.concatenate([high + pltpu.roll(high, 64, 1), low], axis=0).astype(BF16)

    weight_y = [0.0] * ny
    for k in range(1, 7):
        weight_y[k % ny] += LAP_COEF[k]
        weight_y[-k % ny] += LAP_COEF[k]

    def hamilton(stage, c, scale, put):
        coeff = returned(stage, c)
        halo(stage, c, 0).wait_recv()
        halo(stage, c, 1).wait_recv()

        @pl.loop(0, planes)
        def _(z):
            base = rows + z * ny
            centre = [ext[stage, c, base + y] for y in range(ny)]
            v = v_ref[pl.ds(pl.multiple_of(z * ny, ny), ny), :]
            for pair in range(ny // 2):
                part = jnp.dot(
                    coeff, pt[z * (ny // 2) + pair], preferred_element_type=F32
                )
                part = part[:OB] + part[OB:]
                for half in range(2):
                    y = 2 * pair + half
                    f = centre[y]
                    acc = part[:, half * lanes : (half + 1) * lanes]
                    own = v[y : y + 1, :] + (
                        -1.5 * LAP_COEF[0] - CENTRE - 0.5 * weight_y[0]
                    )
                    acc = acc + own * f
                    for k in range(1, 7):
                        both = (
                            ext[stage, c, base + y + ny * k]
                            + ext[stage, c, base + y - ny * k]
                            + pltpu.roll(f, k, 1)
                            + pltpu.roll(f, lanes - k, 1)
                        )
                        acc = acc + (-0.5 * LAP_COEF[k]) * both
                    for k in range(1, ny // 2):
                        acc = acc + (-0.5 * weight_y[k]) * (
                            centre[(y + k) % ny] + centre[(y - k) % ny]
                        )
                    acc = acc + (-0.5 * weight_y[ny // 2]) * centre[(y + ny // 2) % ny]
                    put(z * ny + y, scale * acc)

    @pl.loop(0, chunks)
    def _(c):
        def put(r, value):
            ext[1, c, rows + r] = value

        hamilton(0, c, SIGMA / HALF_WIDTH, put)
        halo(1, c, 0).start()
        halo(1, c, 1).start()
        project(1, c)

    def quarter_copy(c, d):
        other = orb_id(d)
        return pltpu.make_async_remote_copy(
            src_ref=fbuf.at[c, pl.ds(other * quarter, quarter)],
            dst_ref=abuf.at[n_orb - d, c],
            send_sem=a_send.at[c, d],
            recv_sem=a_recv.at[c, n_orb - d],
            device_id=(g, other),
            device_id_type=MESH,
        )

    def quarter_arrival(c, d):
        return pltpu.make_async_remote_copy(
            src_ref=fbuf.at[c, pl.ds(0, quarter)],
            dst_ref=abuf.at[d, c],
            send_sem=a_send.at[c, d],
            recv_sem=a_recv.at[c, d],
            device_id=(g, orb_id(d)),
            device_id_type=MESH,
        )

    @pl.loop(0, chunks)
    def _(c):
        def put(r, value):
            value = value + (-SIGMA * SIGMA_TWO) * ext[0, c, rows + r]
            fbuf[c, r] = value
            out_ref[pl.ds(c * OB * rows + r, OB, stride=rows), :] = value

        hamilton(1, c, 2.0 * SIGMA_TWO / HALF_WIDTH, put)
        for d in range(1, n_orb):
            quarter_copy(c, d).start()
        abuf[0, c] = fbuf[c, pl.ds(o * quarter, quarter)]

    for d in range(1, n_orb):
        @pl.loop(0, chunks)
        def _(c):
            quarter_arrival(c, d).wait_recv()

    per = chunks * OB
    norb = n_orb * per

    @pl.loop(0, n_orb)
    def _(b):
        slot = lax.rem(b - o + n_orb, n_orb)
        place = pl.multiple_of(b * per, per)
        for r in range(quarter):
            block = abuf[slot, :, r].reshape(per, lanes)
            high, low = split(block)
            ah[pl.ds(place, per), r * lanes : (r + 1) * lanes] = high.astype(BF16)
            ah[pl.ds(norb + place, per), r * lanes : (r + 1) * lanes] = low.astype(BF16)

    prod = lax.dot_general(ah[0:norb], ah[...], NT, preferred_element_type=F32)
    gbuf[...] = prod[:, :norb] + prod[:, norb:]
    prod = lax.dot_general(ah[norb:], ah[0:norb], NT, preferred_element_type=F32)
    gbuf[...] += prod

    def rows_copy(d):
        other = orb_id(d)
        return pltpu.make_async_remote_copy(
            src_ref=gbuf.at[pl.ds(pl.multiple_of(other * per, per), per)],
            dst_ref=grecv.at[n_orb - d],
            send_sem=g_send.at[d],
            recv_sem=g_recv.at[n_orb - d],
            device_id=(g, other),
            device_id_type=MESH,
        )

    def rows_arrival(d):
        return pltpu.make_async_remote_copy(
            src_ref=gbuf.at[pl.ds(0, per)],
            dst_ref=grecv.at[d],
            send_sem=g_send.at[d],
            recv_sem=g_recv.at[d],
            device_id=(g, orb_id(d)),
            device_id_type=MESH,
        )

    for d in range(1, n_orb):
        rows_copy(d).start()
    total = gbuf[pl.ds(pl.multiple_of(o * per, per), per)]
    for d in range(1, n_orb):
        rows_arrival(d).wait_recv()
        total = total + grecv[d]
    sbuf[...] = total

    def sum_copy(d):
        return pltpu.make_async_remote_copy(
            src_ref=sbuf,
            dst_ref=srecv.at[n_grid - d],
            send_sem=s_send.at[d],
            recv_sem=s_recv.at[n_grid - d],
            device_id=(grid_id(d), o),
            device_id_type=MESH,
        )

    def sum_arrival(d):
        return pltpu.make_async_remote_copy(
            src_ref=sbuf,
            dst_ref=srecv.at[d],
            send_sem=s_send.at[d],
            recv_sem=s_recv.at[d],
            device_id=(grid_id(d), o),
            device_id_type=MESH,
        )

    @pl.loop(1, n_grid)
    def _(d):
        sum_copy(d).start()

    @pl.loop(1, n_grid)
    def _(d):
        sum_arrival(d).wait_recv()

    total = sbuf[...]
    total = lax.fori_loop(1, n_grid, lambda d, acc: acc + srecv[d], total)
    columns = norb // n_grid
    total = pltpu.roll(total, lax.rem(norb - g * columns, norb), 1)
    gram_ref[...] = total[:, :columns] * (1.0 / (n_grid * rows * lanes))

    @pl.loop(0, chunks)
    def _(c):
        for stage in range(2):
            for side in range(2):
                halo(stage, c, side).wait_send()
            for i in range(4):
                partial_copy(stage, c, i).wait_send()
        for d in range(1, n_orb):
            quarter_copy(c, d).wait_send()

    for d in range(1, n_orb):
        rows_copy(d).wait_send()

    @pl.loop(1, n_grid)
    def _(d):
        sum_copy(d).wait_send()


def on_device(psi_in, v_local, proj_index, proj_value, kb_energy):
    n_grid = lax.axis_size("grid")
    n_orb = lax.axis_size("orb")
    orbitals, planes, ny, nx = psi_in.shape
    rows = planes * ny
    chunks = orbitals // OB
    norb = orbitals * n_orb
    quarter = rows // n_orb
    psi = psi_in.reshape(orbitals * rows, nx)
    v = v_local.reshape(rows, nx)
    index = proj_index.reshape(6, 1, 2 * nx)
    value = proj_value.reshape(6, 8, nx)
    kb = jnp.broadcast_to(jnp.pad(kb_energy.reshape(1, 16), ((0, 0), (64, 48))), (OB, nx))
    dma = pltpu.SemaphoreType.DMA
    vmem = pl.BlockSpec(memory_space=pltpu.VMEM)
    filtered, gram = pl.pallas_call(
        functools.partial(kernel, n_grid, n_orb, ny, planes, chunks),
        out_shape=(
            jax.ShapeDtypeStruct((orbitals * rows, nx), F32),
            jax.ShapeDtypeStruct((orbitals, norb // n_grid), F32),
        ),
        in_specs=[vmem] * 5,
        out_specs=(vmem, vmem),
        scratch_shapes=[
            pltpu.VMEM((2, chunks, 3 * rows, OB, nx), F32),
            pltpu.VMEM((rows, KP, nx), F32),
            pltpu.VMEM((rows // 2, 2 * KP, 2 * nx), BF16),
            pltpu.VMEM((chunks, rows, OB, nx), F32),
            pltpu.VMEM((n_orb, chunks, quarter, OB, nx), F32),
            pltpu.VMEM((2 * norb, quarter * nx), BF16),
            pltpu.VMEM((norb, norb), F32),
            pltpu.VMEM((n_orb, orbitals, norb), F32),
            pltpu.VMEM((orbitals, norb), F32),
            pltpu.VMEM((n_grid, orbitals, norb), F32),
            pltpu.VMEM((2, chunks, OB, nx), F32),
            pltpu.VMEM((2, chunks, 4, OB, nx), F32),
            dma((2, chunks, 2)),
            dma((2, chunks, 2)),
            dma((2, chunks, 4)),
            dma((2, chunks, 4)),
            dma((chunks, n_orb)),
            dma((chunks, n_orb)),
            dma((n_orb,)),
            dma((n_orb,)),
            dma((n_grid,)),
            dma((n_grid,)),
        ],
        compiler_params=pltpu.CompilerParams(
            collective_id=0, has_side_effects=True, vmem_limit_bytes=40 * 1024 * 1024
        ),
        cost_estimate=pl.CostEstimate(
            flops=400_000_000, bytes_accessed=2_000_000, transcendentals=0
        ),
    )(psi, v, index, value, kb)
    return filtered.reshape(psi_in.shape), gram


def solution(mesh):
    placed = (
        P("orb", "grid", None, None),
        P("grid", None, None),
        P("grid", None, None),
        P("grid", None, None, None),
        P("grid", None),
    )
    return jax.shard_map(
        on_device,
        mesh=mesh,
        in_specs=placed,
        out_specs=(P("orb", "grid", None, None), P("orb", "grid")),
        check_vma=False,
    )
```

time: 271 us -> 69.7 us (0.26)
  waiting for transfers between devices: 108 us -> 0 us
  local copies, waits for them, and re-layouts: 76.5 us -> 4.99 us
  Pallas kernels: 0 us -> 63.8 us
  other arithmetic: 46.9 us -> 0 us
  starting transfers between devices: 16.8 us -> 0 us
  between operations: 14.3 us -> 0.66 us
  matrix products: 7.67 us -> 0 us
    all_gather x1 -> x0, waiting for transfers between devices: 65.1 us -> none  [on_device(): lax.all_gather(flattened, 'orb', axis=0, tiled=True)]
    pallas_call x0 -> x1, Pallas kernels: none -> 63.8 us  [on_device(): pl.pallas_call(functools.partial(kernel, n_grid, n_orb, ny, planes, chunk...]
    slice x40 -> x0, local copies, waits for them, and re-layouts: 48.3 us -> none  [the longest x38 48.3 us: hamilton(): jnp.roll(field, offset, axis) + jnp.roll(field, -offset, axis)]
    reduce_scatter x1 -> x0, waiting for transfers between devices: 32 us -> none  [on_device(): lax.psum_scatter(partial_value, 'grid', scatter_dimension=1, tiled=True)]
    scatter-add x2 -> x0, other arithmetic: 21 us -> none  [nonlocal_part(): result = jnp.zeros_like(flattened).at[:, columns].add(contrib)]
    ppermute x12 -> x0, starting transfers between devices: 16.7 us -> none  [the longest x6 16.2 us: with_halo(): lax.ppermute(head, axis, [((i + 1) % count, i) for i in range(count)])]
    sub x1 -> x0, other arithmetic: 13.2 us -> none  [on_device(): (hamilton(first, v_local, proj_index, proj_value, kb_energy) - centre * f...]
    ppermute x12 -> x0, waiting for transfers between devices: 11 us -> none  [the longest x6 10.9 us: with_halo(): lax.ppermute(tail, axis, [(i, (i + 1) % count) for i in range(count)])]
  transfers between devices with their start and end apart: 14 -> 0, of which waited for: 5 -> 0; matrix products, arithmetic and copies ran while one was open for 27% -> 0% of each run, Pallas kernels for 0% -> 0%
where the time goes in v1:
time: 69.7 us; the launch traced here: 69.4 us
  Pallas kernels  63.8 us (92%)
  local copies, waits for them, and re-layouts  4.99 us (7%)
    pallas_call x1, Pallas kernels, on_device(): pl.pallas_call(functools.partial(kernel, n_grid, n_orb, ny, planes, chunk...  63.8 us
    unnamed x12, local copies, waits for them, and re-layouts  4.83 us

profile of v1, /device:TPU:0, one launch (start us, length us, event | category | flops | bytes accessed | tf_op | source)
XLA Modules:
  0.0 69.4 jit_solution(767992388675872700)
XLA Ops:
  0.6 0.0 copy-start.4
  0.6 0.0 copy-start.3
  0.6 0.7 copy-done.4
  1.3 0.1 reshape.26
  1.4 0.1 pad_bitcast_fusion
  1.5 0.0 copy-done.3
  1.5 0.0 copy-start
  1.5 1.1 %copy-done = f32[32,6,8,128]{3,2,1,0:T(8,128)S(1)} copy-done((f32[32,6,8,128]{3,2,1,0:T(8,128)S(1)}, f32[32,6,8,128]{3,2,1,0:T(8,128)}, u32[]{:S(2)}) %copy-start) | copy-done | bytes 786456
  2.6 0.0 copy-start.1
  2.6 0.7 %copy-done.1 = f32[6,8,128]{2,1,0:T(8,128)S(1)} copy-done((f32[6,8,128]{2,1,0:T(8,128)S(1)}, f32[6,8,128]{2,1,0:T(8,128)}, u32[]{:S(2)}) %copy-start.1) | copy-done | bytes 24600
  3.4 0.0 copy-start.2
  3.4 0.7 %copy-done.2 = f32[3,4,4,128]{3,2,1,0:T(4,128)S(1)} copy-done((f32[3,4,4,128]{3,2,1,0:T(4,128)S(1)}, f32[3,4,4,128]{3,2,1,0:T(4,128)}, u32[]{:S(2)}) %copy-start.2) | copy-done | bytes 24600
  4.1 63.8 %shard_map.68 = (f32[1536,128]{1,0:T(8,128)S(1)}, f32[32,16]{1,0:T(8,128)S(1)}) custom-call(f32[1536,128]{1,0:T(8,128)S(1)} %bitcast.8, f32[48,128]{1,0:T(8,128)S(1)} %bitcast.9, s32[6,1,256]{2,1,0:T(1,128)S(1)} %bitcast.11, f32[6,8,128]{2,1,0:T(8,128)S(1)} %bitcast.10, f32[8,128]{1,0:T(8,128)S(1)} %broadcast_in_dim.8.kb_ref), custom_call_target="tpu_custom_call" | custom-call | flops 400000000 | bytes 2000000 | tf_op jit(solution)/shard_map/pallas_call | solution.py:377
  67.9 0.7 copy.7
  68.6 0.9 %copy.9 = f32[32,6,8,128]{3,2,1,0:T(8,128)} copy(f32[32,6,8,128]{3,2,1,0:T(8,128)S(1)} %bitcast.7) | data formatting | bytes 1572864
  (1 shorter events, 0.0 us)
Async XLA Ops:
  0.6 0.7 copy-start.4
  0.6 0.8 %copy-start.3 = (s32[3,4,128]{2,1,0:T(4,128)S(1)}, s32[3,4,128]{2,1,0:T(4,128)}, u32[]{:S(2)}) copy-start(s32[3,4,128]{2,1,0:T(4,128)} %param.7) | copy-start | bytes 18436
  1.5 1.1 %copy-start = (f32[32,6,8,128]{3,2,1,0:T(8,128)S(1)}, f32[32,6,8,128]{3,2,1,0:T(8,128)}, u32[]{:S(2)}) copy-start(f32[32,6,8,128]{3,2,1,0:T(8,128)} %param.5) | copy-start | bytes 2359300
  2.6 0.7 %copy-start.1 = (f32[6,8,128]{2,1,0:T(8,128)S(1)}, f32[6,8,128]{2,1,0:T(8,128)}, u32[]{:S(2)}) copy-start(f32[6,8,128]{2,1,0:T(8,128)} %param.6) | copy-start | bytes 73732
  3.4 0.7 %copy-start.2 = (f32[3,4,4,128]{3,2,1,0:T(4,128)S(1)}, f32[3,4,4,128]{3,2,1,0:T(4,128)}, u32[]{:S(2)}) copy-start(f32[3,4,4,128]{3,2,1,0:T(4,128)} %param.8) | copy-start | bytes 73732

commit v2 on v1

--- a/solution.py
+++ b/solution.py
@@ -36,10 +36,10 @@
 
 def kernel(
     n_grid, n_orb, ny, planes, chunks,
-    psi_ref, v_ref, idx_ref, val_ref, kb_ref,
+    psi_hbm, v_hbm, idx_hbm, val_hbm, kb_hbm,
     out_ref, gram_ref,
-    ext, pf, pt, fbuf, abuf, ah, gbuf, grecv, sbuf, srecv, pay, prec,
-    h_send, h_recv, p_send, p_recv, a_send, a_recv, g_send, g_recv, s_send, s_recv,
+    psi_ref, v_ref, idx_ref, val_ref, kb_ref, con, ext, pf, pt, fbuf, abuf, ah, gbuf, grecv, sbuf, srecv, pay, prec,
+    h_send, h_recv, p_send, p_recv, a_send, a_recv, g_send, g_recv, s_send, s_recv, in_sem, psi_sem,
 ):
     rows = ny * planes
     quarter = rows // n_orb
@@ -53,6 +53,24 @@
     def orb_id(d):
         return lax.rem(o + d, n_orb)
 
+    def psi_copy(c):
+        part = pl.ds(c * OB * rows, OB * rows)
+        return pltpu.make_async_copy(psi_hbm.at[part], psi_ref.at[part], psi_sem.at[c])
+
+    small = [
+        pltpu.make_async_copy(src, dst, in_sem.at[i])
+        for i, (src, dst) in enumerate(
+            ((idx_hbm, idx_ref), (val_hbm, val_ref), (kb_hbm, kb_ref), (v_hbm, v_ref))
+        )
+    ]
+
+    @pl.loop(0, chunks)
+    def _(c):
+        psi_copy(c).start()
+
+    for copy in small:
+        copy.start()
+
     barrier = pltpu.get_barrier_semaphore()
 
     @pl.loop(1, n_grid)
@@ -64,9 +82,14 @@
 
     @pl.loop(0, chunks)
     def _(c):
+        psi_copy(c).wait()
+
         @pl.loop(0, rows, unroll=8)
         def _(r):
             ext[0, c, rows + r] = psi_ref[pl.ds(c * OB * rows + r, OB, stride=rows), :]
+
+    for copy in small:
+        copy.wait()
 
     pl.semaphore_wait(barrier, n_grid - 1 + n_orb - 1)
 
@@ -90,10 +113,16 @@
             device_id_type=MESH,
         )
 
-    @pl.loop(0, chunks)
-    def _(c):
-        halo(0, c, 0).start()
-        halo(0, c, 1).start()
+    def halo_start(stage, c):
+        halo(stage, c, 0).start()
+        halo(stage, c, 1).start()
+
+    def halo_left(stage, c):
+        halo(stage, c, 0).wait_send()
+        halo(stage, c, 1).wait_send()
+
+    for c in range(2):
+        halo_start(0, c)
 
     pf[:, 48:KP, :] = jnp.zeros((rows, KP - 48, lanes), F32)
 
@@ -129,24 +158,41 @@
 
     lane = lax.broadcasted_iota(jnp.int32, (OB, lanes), 1)
 
-    def project(stage, c):
+    energies = jnp.zeros((OB, lanes), F32)
+    for a in range(4):
+        for m in range(4):
+            energies = jnp.where(lane == 64 + 4 * a + m, kb_ref[a : a + 1, m : m + 1], energies)
+
+    def project(stage, first, count):
         def step(h, acc):
             both = jnp.concatenate(
-                [ext[stage, c, rows + 2 * h], ext[stage, c, rows + 2 * h + 1]], axis=1
+                [
+                    jnp.concatenate(
+                        [ext[stage, first + i, rows + 2 * h + j] for i in range(count)], axis=0
+                    )
+                    for j in range(2)
+                ],
+                axis=1,
             )
             high, low = split(both)
             left = jnp.concatenate([high, low], axis=0).astype(BF16)
             return acc + lax.dot_general(left, pt[h], NT, preferred_element_type=F32)
 
-        acc = lax.fori_loop(0, rows // 2, step, jnp.zeros((2 * OB, lanes), F32), unroll=4)
-        total = acc[:OB] + acc[OB:] + pltpu.roll(acc[:OB], 64, 1)
-        pay[stage, c] = jnp.where(lane < 48, total, kb_ref[...])
-        for i in range(4):
-            partial_copy(stage, c, i).start()
-
-    @pl.loop(0, chunks)
-    def _(c):
-        project(0, c)
+        most = count * OB
+        acc = lax.fori_loop(0, rows // 2, step, jnp.zeros((2 * most, lanes), F32), unroll=4)
+        total = acc[:most] + acc[most:] + pltpu.roll(acc[:most], 64, 1)
+        for i in range(count):
+            pay[stage, first + i] = jnp.where(
+                lane < 48, total[i * OB : (i + 1) * OB], energies
+            )
+            for partner in range(4):
+                partial_copy(stage, first + i, partner).start()
+
+    halo_left(0, 0)
+    halo_start(0, 2)
+    project(0, 0, chunks)
+    halo_left(0, 1)
+    halo_start(0, 3)
 
     def returned(stage, c):
         for i in range(4):
@@ -167,7 +213,24 @@
         )
         total = jnp.where(lane < 48, total * energy, 0.0)
         high, low = split(total)
-        return jnp.concatenate([high + pltpu.roll(high, 64, 1), low], axis=0).astype(BF16)
+        return high + pltpu.roll(high, 64, 1), low
+
+    def contribute(stage, first, count):
+        parts = [returned(stage, first + i) for i in range(count)]
+        coeff = jnp.concatenate(
+            [high for high, _ in parts] + [low for _, low in parts], axis=0
+        ).astype(BF16)
+        most = count * OB
+
+        @pl.loop(0, rows // 2, unroll=4)
+        def _(h):
+            part = jnp.dot(coeff, pt[h], preferred_element_type=F32)
+            part = part[:most] + part[most:]
+            for i in range(count):
+                for half in range(2):
+                    con[first + i, 2 * h + half] = part[
+                        i * OB : (i + 1) * OB, half * lanes : (half + 1) * lanes
+                    ]
 
     weight_y = [0.0] * ny
     for k in range(1, 7):
@@ -175,7 +238,6 @@
         weight_y[-k % ny] += LAP_COEF[k]
 
     def hamilton(stage, c, scale, put):
-        coeff = returned(stage, c)
         halo(stage, c, 0).wait_recv()
         halo(stage, c, 1).wait_recv()
 
@@ -184,43 +246,41 @@
             base = rows + z * ny
             centre = [ext[stage, c, base + y] for y in range(ny)]
             v = v_ref[pl.ds(pl.multiple_of(z * ny, ny), ny), :]
-            for pair in range(ny // 2):
-                part = jnp.dot(
-                    coeff, pt[z * (ny // 2) + pair], preferred_element_type=F32
+            for y in range(ny):
+                f = centre[y]
+                acc = con[c, z * ny + y]
+                own = v[y : y + 1, :] + (
+                    -1.5 * LAP_COEF[0] - CENTRE - 0.5 * weight_y[0]
                 )
-                part = part[:OB] + part[OB:]
-                for half in range(2):
-                    y = 2 * pair + half
-                    f = centre[y]
-                    acc = part[:, half * lanes : (half + 1) * lanes]
-                    own = v[y : y + 1, :] + (
-                        -1.5 * LAP_COEF[0] - CENTRE - 0.5 * weight_y[0]
+                acc = acc + own * f
+                for k in range(1, 7):
+                    both = (
+                        ext[stage, c, base + y + ny * k]
+                        + ext[stage, c, base + y - ny * k]
+                        + pltpu.roll(f, k, 1)
+                        + pltpu.roll(f, lanes - k, 1)
                     )
-                    acc = acc + own * f
-                    for k in range(1, 7):
-                        both = (
-                            ext[stage, c, base + y + ny * k]
-                            + ext[stage, c, base + y - ny * k]
-                            + pltpu.roll(f, k, 1)
-                            + pltpu.roll(f, lanes - k, 1)
-                        )
-                        acc = acc + (-0.5 * LAP_COEF[k]) * both
-                    for k in range(1, ny // 2):
-                        acc = acc + (-0.5 * weight_y[k]) * (
-                            centre[(y + k) % ny] + centre[(y - k) % ny]
-                        )
-                    acc = acc + (-0.5 * weight_y[ny // 2]) * centre[(y + ny // 2) % ny]
-                    put(z * ny + y, scale * acc)
-
-    @pl.loop(0, chunks)
-    def _(c):
-        def put(r, value):
-            ext[1, c, rows + r] = value
-
-        hamilton(0, c, SIGMA / HALF_WIDTH, put)
-        halo(1, c, 0).start()
-        halo(1, c, 1).start()
-        project(1, c)
+                    acc = acc + (-0.5 * LAP_COEF[k]) * both
+                for k in range(1, ny // 2):
+                    acc = acc + (-0.5 * weight_y[k]) * (
+                        centre[(y + k) % ny] + centre[(y - k) % ny]
+                    )
+                acc = acc + (-0.5 * weight_y[ny // 2]) * centre[(y + ny // 2) % ny]
+                put(z * ny + y, scale * acc)
+
+    contribute(0, 0, chunks)
+
+    @pl.loop(0, chunks // 2)
+    def _(pair):
+        @pl.loop(2 * pair, 2 * pair + 2)
+        def _(c):
+            def put(r, value):
+                ext[1, c, rows + r] = value
+
+            hamilton(0, c, SIGMA / HALF_WIDTH, put)
+            halo_start(1, c)
+
+        project(1, 2 * pair, 2)
 
     def quarter_copy(c, d):
         other = orb_id(d)
@@ -243,17 +303,21 @@
             device_id_type=MESH,
         )
 
-    @pl.loop(0, chunks)
-    def _(c):
-        def put(r, value):
-            value = value + (-SIGMA * SIGMA_TWO) * ext[0, c, rows + r]
-            fbuf[c, r] = value
-            out_ref[pl.ds(c * OB * rows + r, OB, stride=rows), :] = value
-
-        hamilton(1, c, 2.0 * SIGMA_TWO / HALF_WIDTH, put)
-        for d in range(1, n_orb):
-            quarter_copy(c, d).start()
-        abuf[0, c] = fbuf[c, pl.ds(o * quarter, quarter)]
+    @pl.loop(0, chunks // 2)
+    def _(pair):
+        contribute(1, 2 * pair, 2)
+
+        @pl.loop(2 * pair, 2 * pair + 2)
+        def _(c):
+            def put(r, value):
+                value = value + (-SIGMA * SIGMA_TWO) * ext[0, c, rows + r]
+                fbuf[c, r] = value
+                out_ref[pl.ds(c * OB * rows + r, OB, stride=rows), :] = value
+
+            hamilton(1, c, 2.0 * SIGMA_TWO / HALF_WIDTH, put)
+            for d in range(1, n_orb):
+                quarter_copy(c, d).start()
+            abuf[0, c] = fbuf[c, pl.ds(o * quarter, quarter)]
 
     for d in range(1, n_orb):
         @pl.loop(0, chunks)
@@ -339,17 +403,19 @@
     total = lax.fori_loop(1, n_grid, lambda d, acc: acc + srecv[d], total)
     columns = norb // n_grid
     total = pltpu.roll(total, lax.rem(norb - g * columns, norb), 1)
-    gram_ref[...] = total[:, :columns] * (1.0 / (n_grid * rows * lanes))
+    gram_ref[...] = total.T[:columns] * (1.0 / (n_grid * rows * lanes))
 
     @pl.loop(0, chunks)
     def _(c):
+        halo_left(1, c)
         for stage in range(2):
-            for side in range(2):
-                halo(stage, c, side).wait_send()
             for i in range(4):
                 partial_copy(stage, c, i).wait_send()
         for d in range(1, n_orb):
             quarter_copy(c, d).wait_send()
+
+    for c in range(2, 4):
+        halo_left(0, c)
 
     for d in range(1, n_orb):
         rows_copy(d).wait_send()
@@ -371,18 +437,24 @@
     v = v_local.reshape(rows, nx)
     index = proj_index.reshape(6, 1, 2 * nx)
     value = proj_value.reshape(6, 8, nx)
-    kb = jnp.broadcast_to(jnp.pad(kb_energy.reshape(1, 16), ((0, 0), (64, 48))), (OB, nx))
     dma = pltpu.SemaphoreType.DMA
     vmem = pl.BlockSpec(memory_space=pltpu.VMEM)
+    hbm = pl.BlockSpec(memory_space=pltpu.HBM)
     filtered, gram = pl.pallas_call(
         functools.partial(kernel, n_grid, n_orb, ny, planes, chunks),
         out_shape=(
             jax.ShapeDtypeStruct((orbitals * rows, nx), F32),
-            jax.ShapeDtypeStruct((orbitals, norb // n_grid), F32),
+            jax.ShapeDtypeStruct((norb // n_grid, orbitals), F32),
         ),
-        in_specs=[vmem] * 5,
+        in_specs=[hbm] * 5,
         out_specs=(vmem, vmem),
         scratch_shapes=[
+            pltpu.VMEM(psi.shape, F32),
+            pltpu.VMEM(v.shape, F32),
+            pltpu.VMEM(index.shape, jnp.int32),
+            pltpu.VMEM(value.shape, F32),
+            pltpu.VMEM(kb_energy.shape, F32),
+            pltpu.VMEM((chunks, rows, OB, nx), F32),
             pltpu.VMEM((2, chunks, 3 * rows, OB, nx), F32),
             pltpu.VMEM((rows, KP, nx), F32),
             pltpu.VMEM((rows // 2, 2 * KP, 2 * nx), BF16),
@@ -405,15 +477,17 @@
             dma((n_orb,)),
             dma((n_grid,)),
             dma((n_grid,)),
+            dma((4,)),
+            dma((chunks,)),
         ],
         compiler_params=pltpu.CompilerParams(
-            collective_id=0, has_side_effects=True, vmem_limit_bytes=40 * 1024 * 1024
+            collective_id=0, has_side_effects=True, vmem_limit_bytes=62 * 1024 * 1024
         ),
         cost_estimate=pl.CostEstimate(
             flops=400_000_000, bytes_accessed=2_000_000, transcendentals=0
         ),
-    )(psi, v, index, value, kb)
-    return filtered.reshape(psi_in.shape), gram
+    )(psi, v, index, value, kb_energy)
+    return filtered.reshape(psi_in.shape), gram.T
 
 
 def solution(mesh):

time: 69.7 us -> 71.8 us (1.030)
  Pallas kernels: 63.8 us -> 68.3 us
  local copies, waits for them, and re-layouts: 4.99 us -> 2.67 us
    pallas_call x1, Pallas kernels: 63.8 us -> 68.3 us  [on_device(): pl.pallas_call(functools.partial(kernel, n_grid, n_orb, ny, planes, chunk...]
    unnamed x12 -> x4, local copies, waits for them, and re-layouts: 4.83 us -> 2.67 us
where the time goes in v2:
time: 71.8 us; the launch traced here: 71.6 us
  Pallas kernels  68.3 us (95%)
  local copies, waits for them, and re-layouts  2.67 us (4%)
    pallas_call x1, Pallas kernels, on_device(): pl.pallas_call(functools.partial(kernel, n_grid, n_orb, ny, planes, chunk...  68.3 us
    unnamed x4, local copies, waits for them, and re-layouts  2.67 us

profile of v2, /device:TPU:0, one launch (start us, length us, event | category | flops | bytes accessed | tf_op | source)
XLA Modules:
  0.0 71.6 jit_solution(3206194436521897815)
XLA Ops:
  0.6 68.3 %shard_map.68 = (f32[1536,128]{1,0:T(8,128)}, f32[16,32]{1,0:T(8,128)}) custom-call(f32[1536,128]{1,0:T(8,128)} %bitcast.8, f32[48,128]{1,0:T(8,128)} %bitcast.9, s32[6,1,256]{2,1,0:T(1,128)} %bitcast.11, f32[6,8,128]{2,1,0:T(8,128)} %bitcast.10, f32[4,4]{1,0:T(4,128)} %kb_hbm.1), custom_call_target="tpu_custom_call" | custom-call | flops 400000000 | bytes 2000000 | tf_op jit(solution)/shard_map/pallas_call | solution.py:443
  68.9 0.0 copy-start
  68.9 2.1 %copy.9 = f32[32,6,8,128]{3,2,1,0:T(8,128)} copy(f32[32,6,8,128]{3,2,1,0:T(8,128)} %bitcast.6) | data formatting | bytes 1572864
  71.0 0.0 copy-done
  71.0 0.6 copy.10
Async XLA Ops:
  68.9 2.1 %copy-start = (f32[16,32]{1,0:T(8,128)S(1)}, f32[16,32]{1,0:T(8,128)}, u32[]{:S(2)}) copy-start(f32[16,32]{1,0:T(8,128)} %get-tuple-element.5) | copy-start | bytes 6148

commit v3 on v2

--- a/solution.py
+++ b/solution.py
@@ -37,9 +37,9 @@
 def kernel(
     n_grid, n_orb, ny, planes, chunks,
     psi_hbm, v_hbm, idx_hbm, val_hbm, kb_hbm,
-    out_ref, gram_ref,
-    psi_ref, v_ref, idx_ref, val_ref, kb_ref, con, ext, pf, pt, fbuf, abuf, ah, gbuf, grecv, sbuf, srecv, pay, prec,
-    h_send, h_recv, p_send, p_recv, a_send, a_recv, g_send, g_recv, s_send, s_recv, in_sem, psi_sem,
+    out_hbm, gram_ref,
+    out_ref,    psi_ref, v_ref, idx_ref, val_ref, kb_ref, con, ext, pf, pt, fbuf, abuf, ah, gbuf, grecv, sbuf, srecv, pay, prec,
+    h_send, h_recv, p_send, p_recv, a_send, a_recv, g_send, g_recv, s_send, s_recv, in_sem, psi_sem, out_sem,
 ):
     rows = ny * planes
     quarter = rows // n_orb
@@ -121,8 +121,11 @@
         halo(stage, c, 0).wait_send()
         halo(stage, c, 1).wait_send()
 
-    for c in range(2):
-        halo_start(0, c)
+    def advance(k):
+        halo_left((k - 1) // chunks, (k - 1) % chunks)
+        halo_start(k // chunks, k % chunks)
+
+    halo_start(0, 0)
 
     pf[:, 48:KP, :] = jnp.zeros((rows, KP - 48, lanes), F32)
 
@@ -150,6 +153,8 @@
         dense = dense + lax.dot_general(left, hot, NT, preferred_element_type=F32)
         pf[:, pl.ds(pl.multiple_of(q * 8, 8), 8), :] = dense.reshape(rows, 8, lanes)
 
+    advance(1)
+
     @pl.loop(0, rows // 2, unroll=2)
     def _(h):
         both = jnp.concatenate([pf[2 * h], pf[2 * h + 1]], axis=1)
@@ -188,11 +193,8 @@
             for partner in range(4):
                 partial_copy(stage, first + i, partner).start()
 
-    halo_left(0, 0)
-    halo_start(0, 2)
     project(0, 0, chunks)
-    halo_left(0, 1)
-    halo_start(0, 3)
+    advance(2)
 
     def returned(stage, c):
         for i in range(4):
@@ -270,17 +272,22 @@
 
     contribute(0, 0, chunks)
 
-    @pl.loop(0, chunks // 2)
-    def _(pair):
-        @pl.loop(2 * pair, 2 * pair + 2)
-        def _(c):
-            def put(r, value):
-                ext[1, c, rows + r] = value
-
-            hamilton(0, c, SIGMA / HALF_WIDTH, put)
-            halo_start(1, c)
-
-        project(1, 2 * pair, 2)
+    def first_stage(c):
+        def put(r, value):
+            ext[1, c, rows + r] = value
+
+        hamilton(0, c, SIGMA / HALF_WIDTH, put)
+
+    first_stage(0)
+    advance(3)
+    first_stage(1)
+    project(1, 0, 2)
+    advance(4)
+    first_stage(2)
+    first_stage(3)
+    project(1, 2, 2)
+    advance(5)
+    contribute(1, 0, 2)
 
     def quarter_copy(c, d):
         other = orb_id(d)
@@ -303,21 +310,29 @@
             device_id_type=MESH,
         )
 
-    @pl.loop(0, chunks // 2)
-    def _(pair):
-        contribute(1, 2 * pair, 2)
-
-        @pl.loop(2 * pair, 2 * pair + 2)
-        def _(c):
-            def put(r, value):
-                value = value + (-SIGMA * SIGMA_TWO) * ext[0, c, rows + r]
-                fbuf[c, r] = value
-                out_ref[pl.ds(c * OB * rows + r, OB, stride=rows), :] = value
-
-            hamilton(1, c, 2.0 * SIGMA_TWO / HALF_WIDTH, put)
-            for d in range(1, n_orb):
-                quarter_copy(c, d).start()
-            abuf[0, c] = fbuf[c, pl.ds(o * quarter, quarter)]
+    def out_copy(c):
+        part = pl.ds(c * OB * rows, OB * rows)
+        return pltpu.make_async_copy(out_ref.at[part], out_hbm.at[part], out_sem.at[c])
+
+    def second_stage(c):
+        def put(r, value):
+            value = value + (-SIGMA * SIGMA_TWO) * ext[0, c, rows + r]
+            fbuf[c, r] = value
+            out_ref[pl.ds(c * OB * rows + r, OB, stride=rows), :] = value
+
+        hamilton(1, c, 2.0 * SIGMA_TWO / HALF_WIDTH, put)
+        for d in range(1, n_orb):
+            quarter_copy(c, d).start()
+        out_copy(c).start()
+        abuf[0, c] = fbuf[c, pl.ds(o * quarter, quarter)]
+
+    second_stage(0)
+    advance(6)
+    second_stage(1)
+    advance(7)
+    contribute(1, 2, 2)
+    second_stage(2)
+    second_stage(3)
 
     for d in range(1, n_orb):
         @pl.loop(0, chunks)
@@ -407,15 +422,14 @@
 
     @pl.loop(0, chunks)
     def _(c):
-        halo_left(1, c)
+        out_copy(c).wait()
         for stage in range(2):
             for i in range(4):
                 partial_copy(stage, c, i).wait_send()
         for d in range(1, n_orb):
             quarter_copy(c, d).wait_send()
 
-    for c in range(2, 4):
-        halo_left(0, c)
+    halo_left(1, chunks - 1)
 
     for d in range(1, n_orb):
         rows_copy(d).wait_send()
@@ -447,8 +461,9 @@
             jax.ShapeDtypeStruct((norb // n_grid, orbitals), F32),
         ),
         in_specs=[hbm] * 5,
-        out_specs=(vmem, vmem),
+        out_specs=(hbm, vmem),
         scratch_shapes=[
+            pltpu.VMEM(psi.shape, F32),
             pltpu.VMEM(psi.shape, F32),
             pltpu.VMEM(v.shape, F32),
             pltpu.VMEM(index.shape, jnp.int32),
@@ -479,6 +494,7 @@
             dma((n_grid,)),
             dma((4,)),
             dma((chunks,)),
+            dma((chunks,)),
         ],
         compiler_params=pltpu.CompilerParams(
             collective_id=0, has_side_effects=True, vmem_limit_bytes=62 * 1024 * 1024

time: 71.8 us -> 66.8 us (0.930)
  Pallas kernels: 68.3 us -> 63.3 us
    pallas_call x1, Pallas kernels: 68.3 us -> 63.3 us  [on_device(): pl.pallas_call(functools.partial(kernel, n_grid, n_orb, ny, planes, chunk...]
where the time goes in v3:
time: 66.8 us; the launch traced here: 66.6 us
  Pallas kernels  63.3 us (95%)
  local copies, waits for them, and re-layouts  2.67 us (4%)
    pallas_call x1, Pallas kernels, on_device(): pl.pallas_call(functools.partial(kernel, n_grid, n_orb, ny, planes, chunk...  63.3 us
    unnamed x4, local copies, waits for them, and re-layouts  2.67 us

profile of v3, /device:TPU:0, one launch (start us, length us, event | category | flops | bytes accessed | tf_op | source)
XLA Modules:
  0.0 66.6 jit_solution(13930902098189181110)
XLA Ops:
  0.6 63.3 %shard_map.68 = (f32[1536,128]{1,0:T(8,128)}, f32[16,32]{1,0:T(8,128)}) custom-call(f32[1536,128]{1,0:T(8,128)} %bitcast.8, f32[48,128]{1,0:T(8,128)} %bitcast.9, s32[6,1,256]{2,1,0:T(1,128)} %bitcast.11, f32[6,8,128]{2,1,0:T(8,128)} %bitcast.10, f32[4,4]{1,0:T(4,128)} %kb_hbm.1), custom_call_target="tpu_custom_call" | custom-call | flops 400000000 | bytes 2000000 | tf_op jit(solution)/shard_map/pallas_call | solution.py:457
  63.9 0.0 copy-start
  63.9 2.1 %copy.9 = f32[32,6,8,128]{3,2,1,0:T(8,128)} copy(f32[32,6,8,128]{3,2,1,0:T(8,128)} %bitcast.6) | data formatting | bytes 1572864
  66.0 0.0 copy-done
  66.0 0.6 copy.10
Async XLA Ops:
  63.9 2.1 %copy-start = (f32[16,32]{1,0:T(8,128)S(1)}, f32[16,32]{1,0:T(8,128)}, u32[]{:S(2)}) copy-start(f32[16,32]{1,0:T(8,128)} %get-tuple-element.5) | copy-start | bytes 6148

commit v4 on v3

--- a/solution.py
+++ b/solution.py
@@ -80,17 +80,14 @@
     for d in range(1, n_orb):
         pl.semaphore_signal(barrier, inc=1, device_id=(g, orb_id(d)), device_id_type=MESH)
 
-    @pl.loop(0, chunks)
-    def _(c):
+    def stage_in(c):
         psi_copy(c).wait()
 
         @pl.loop(0, rows, unroll=8)
         def _(r):
             ext[0, c, rows + r] = psi_ref[pl.ds(c * OB * rows + r, OB, stride=rows), :]
 
-    for copy in small:
-        copy.wait()
-
+    stage_in(0)
     pl.semaphore_wait(barrier, n_grid - 1 + n_orb - 1)
 
     def halo(stage, c, side):
@@ -126,6 +123,9 @@
         halo_start(k // chunks, k % chunks)
 
     halo_start(0, 0)
+    pl.loop(1, chunks)(stage_in)
+    for copy in small:
+        copy.wait()
 
     pf[:, 48:KP, :] = jnp.zeros((rows, KP - 48, lanes), F32)
 
@@ -352,10 +352,8 @@
             ah[pl.ds(place, per), r * lanes : (r + 1) * lanes] = high.astype(BF16)
             ah[pl.ds(norb + place, per), r * lanes : (r + 1) * lanes] = low.astype(BF16)
 
-    prod = lax.dot_general(ah[0:norb], ah[...], NT, preferred_element_type=F32)
-    gbuf[...] = prod[:, :norb] + prod[:, norb:]
-    prod = lax.dot_general(ah[norb:], ah[0:norb], NT, preferred_element_type=F32)
-    gbuf[...] += prod
+    prod = lax.dot_general(ah[...], ah[0:norb], NT, preferred_element_type=F32)
+    gbuf[...] = prod[:norb] + prod[norb:] + prod[norb:].T
 
     def rows_copy(d):
         other = orb_id(d)

time: 66.8 us -> 66.5 us (level)
  no operation moved by 1% of the time
where the time goes in v4:
time: 66.5 us; the launch traced here: 66.3 us
  Pallas kernels  63 us (95%)
  local copies, waits for them, and re-layouts  2.67 us (4%)
    pallas_call x1, Pallas kernels, on_device(): pl.pallas_call(functools.partial(kernel, n_grid, n_orb, ny, planes, chunk...  63 us
    unnamed x4, local copies, waits for them, and re-layouts  2.67 us

profile of v4, /device:TPU:0, one launch (start us, length us, event | category | flops | bytes accessed | tf_op | source)
XLA Modules:
  0.0 66.3 jit_solution(3036212760212232901)
XLA Ops:
  0.6 63.0 %shard_map.68 = (f32[1536,128]{1,0:T(8,128)}, f32[16,32]{1,0:T(8,128)}) custom-call(f32[1536,128]{1,0:T(8,128)} %bitcast.8, f32[48,128]{1,0:T(8,128)} %bitcast.9, s32[6,1,256]{2,1,0:T(1,128)} %bitcast.11, f32[6,8,128]{2,1,0:T(8,128)} %bitcast.10, f32[4,4]{1,0:T(4,128)} %kb_hbm.1), custom_call_target="tpu_custom_call" | custom-call | flops 400000000 | bytes 2000000 | tf_op jit(solution)/shard_map/pallas_call | solution.py:455
  63.7 0.0 copy-start
  63.7 2.1 %copy.9 = f32[32,6,8,128]{3,2,1,0:T(8,128)} copy(f32[32,6,8,128]{3,2,1,0:T(8,128)} %bitcast.6) | data formatting | bytes 1572864
  65.7 0.0 copy-done
  65.7 0.6 copy.10
Async XLA Ops:
  63.7 2.1 %copy-start = (f32[16,32]{1,0:T(8,128)S(1)}, f32[16,32]{1,0:T(8,128)}, u32[]{:S(2)}) copy-start(f32[16,32]{1,0:T(8,128)} %get-tuple-element.5) | copy-start | bytes 6148
